TPU v7x, 32 devices: a whole 2x2x4 slice. The times are simulated.
32 devices in a mesh: groups: 2 (over y), dp: 4 (over x, core), ctx: 4 (over z).
Axes of the slice: x: 2, y: 2, z: 4, core: 2. Of those that a mesh axis runs over, the one named last changes fastest.
Arguments:
- normed_input: bfloat16 [8, 1024, 4096], P(('groups', 'dp'), 'ctx'), parts along dimension 0, may hold values from -6 to 6
- query_weight: bfloat16 [4096, 1024], P(('dp', 'ctx')), may hold values from -0.09375 to 0.09375
- key_vectors: bfloat16 [8, 1024, 1024], P(('groups', 'dp'), 'ctx'), parts along dimension 0, may hold values from -6 to 6
- value_vectors: bfloat16 [8, 1024, 1024], P(('groups', 'dp'), 'ctx'), parts along dimension 0, may hold values from -6 to 6
- input_gate: float32 [8, 4, 1024], P(('groups', 'dp'), None, 'ctx'), parts along dimension 0, may hold values from -16 to 210
- forget_gate: float32 [8, 4, 1024], P(('groups', 'dp'), None, 'ctx'), parts along dimension 0
- resets: int32 [8, 1024], P(('groups', 'dp'), 'ctx'), parts along dimension 0, may hold values 0 or 1
Outputs:
- hidden: bfloat16 [8, 1024, 1024], P(('groups', 'dp'), 'ctx'), parts along dimension 0
There are 2 independent parts, one for each index of `groups`. A program takes and returns all parts, laid end to end along the dimension named above; an argument that names none is the same for every part. Nothing has to cross between parts.
Inputs may be any that keep to these rules, and one draw needn't show every extreme that they name: `resets`: 1 where a new document begins at that position.
All inputs are finite; a program needn't handle non-finite values. No bound on the sum of `resets` on one device may be relied on, other than what follows from the above.
Results may differ from a plain program's by a relative error of at most 0.009.
Values may be sent and summed in bfloat16 or wider, within the bound.
A program may use at most 128 MiB of HBM per device.

v0:
```python
import functools

import jax
import jax.numpy as jnp
from jax import lax
from jax.experimental import pallas as pl
from jax.experimental.pallas import tpu as pltpu
from jax.sharding import PartitionSpec as P

very_low = -1e30
shared_columns = 384
pieces = 4
early = 2
lag_across, lag_over, lag_over_across, lag_mate, lag_mate_across = 2, 2, 4, 5, 7
MESH = pl.DeviceIdType.MESH


def dot(a, b, dims=((1,), (0,))):
    return lax.dot_general(a, b, (dims, ((), ())), preferred_element_type=jnp.float32)


def kernel(
    spread, Z, heads, x_hbm, w_hbm, k_hbm, v_hbm, ig_hbm, fg_hbm, rs_hbm, out_ref,
    gates, flags, xv, kv, vv, wown, wbuf, acc, prob, stack, cols, imax_scr, own_mem, own_info,
    mem_in, info_in, mem_out, info_out,
    lsem, zsend, zrecv, xsend, xrecv, esend, erecv, ysend, yrecv, csend, crecv, ssend, srecv,
):
    y = lax.axis_index("groups")
    d = lax.axis_index("dp")
    z = lax.axis_index("ctx")
    x, c = d // 2, d % 2
    up, down = (y, d, z + 1), (y, d, z - 1)
    across = (y, (1 - x) * 2 + c, z)
    over = (1 - y, d, z)
    mate = (y, x * 2 + 1 - c, z)
    length, features = xv.shape
    dk = kv.shape[1] // heads
    dv = vv.shape[1] // heads
    factor = dk ** (-0.5)
    width = acc.shape[1]
    rows = wbuf.shape[1]
    A = shared_columns

    local = [
        pltpu.make_async_copy(ig_hbm.at[0], gates.at[0, 0:heads], lsem.at[4]),
        pltpu.make_async_copy(fg_hbm.at[0], gates.at[1, 0:heads], lsem.at[5]),
        pltpu.make_async_copy(rs_hbm, flags, lsem.at[6]),
        pltpu.make_async_copy(k_hbm.at[0], kv, lsem.at[0]),
        pltpu.make_async_copy(v_hbm.at[0], vv, lsem.at[1]),
        pltpu.make_async_copy(x_hbm.at[0], xv, lsem.at[2]),
        pltpu.make_async_copy(w_hbm, wown, lsem.at[3]),
    ]
    for one in local:
        one.start()

    barrier = pltpu.get_barrier_semaphore()

    def greet(device):
        pl.semaphore_signal(barrier, inc=1, device_id=device, device_id_type=MESH)

    @pl.when(z < Z - 1)
    def _():
        greet(up)

    @pl.when(z > 0)
    def _():
        greet(down)

    base = 0
    if spread:
        for device in (across, over, mate):
            greet(device)
        base = 3
    pl.semaphore_wait(
        barrier, base + jnp.where(z > 0, 1, 0) + jnp.where(z < Z - 1, 1, 0)
    )

    B = width - 2 * A

    def columns(part):
        if part == 0:
            return pl.ds(pl.multiple_of(y * A, 128), A + B)
        if part == 1:
            return pl.ds(pl.multiple_of(y * (A + B), 128), A)
        return pl.ds(pl.multiple_of((1 - y) * (A + B), 128), A)

    high = rows // pieces

    def shard(xx, cc, zz):
        return (xx * 2 + cc) * Z + zz

    def remote(xx, cc, zz, p, part, send, recv, device, own=False):
        at = pl.ds(p * high if isinstance(p, int) else pl.multiple_of(p * high, 16), high)
        there = wbuf.at[shard(xx, cc, zz), at, columns(part)]
        here = w_hbm.at[at, columns(part)] if own else there
        return pltpu.make_async_remote_copy(
            src_ref=here, dst_ref=there, send_sem=send, recv_sem=recv,
            device_id=device, device_id_type=MESH,
        )

    def z_copy(way, zz, p, own=False):
        device = up if way == 0 else down
        return remote(x, c, zz, p, 0, zsend.at[way], zrecv.at[zz, p], device, own)

    def x_copy(xx, zz, p, own=False):
        return remote(xx, c, zz, p, 0, xsend.at[0], xrecv.at[zz, p], across, own)

    def e_copy(xx, p, own=False):
        return remote(xx, c, z, p, 2, esend.at[0], erecv.at[p], across, own)

    def y_copy(xx, zz, p, part):
        return remote(xx, c, zz, p, part, ysend.at[xx], yrecv.at[xx, zz, p], over)

    def c_copy(xx, cc, zz, p, part, own=False):
        return remote(
            xx, cc, zz, p, part, csend.at[0], crecv.at[xx, zz, p, part // 2], mate, own
        )

    if spread:
        for p in range(pieces):
            @pl.when(z < Z - 1)
            def _():
                z_copy(0, z, p, True).start()

            @pl.when(z > 0)
            def _():
                z_copy(1, z, p, True).start()

            x_copy(x, z, p, True).start()
            if p >= pieces - early:
                e_copy(x, p, True).start()
        for p in range(pieces):
            for part in (0, 2):
                c_copy(x, c, z, p, part, True).start()

    for one in local[:3]:
        one.wait()

    f = gates[1, 0:heads, :]
    stack[...] = jnp.zeros_like(stack)
    stack[0:heads, :] = jnp.minimum(f, 0.0) - jnp.log1p(jnp.exp(-jnp.abs(f)))
    stack[4:5, :] = flags[...].astype(jnp.float32)
    run = stack[0:8, :]
    lane = lax.broadcasted_iota(jnp.int32, run.shape, 1)
    hop = 1
    while hop < length:
        run = run + jnp.where(lane >= hop, pltpu.roll(run, hop, 1), 0.0)
        hop *= 2
    stack[0:8, :] = run
    stack[8:8 + heads, :] = gates[0, 0:heads, :]
    cols[...] = stack[...].T

    def row(at):
        return stack[at:at + 1, :]

    def col(at):
        return cols[:, at:at + 1]

    def last(at):
        return stack[at:at + 1, length - 1:length]

    def own_state(h):
        end_row = jnp.where(row(4) == last(4), last(h) - row(h) + row(8 + h), very_low)
        top = jnp.max(end_row, axis=1, keepdims=True)
        end_col = jnp.where(col(4) == last(4), last(h) - col(h) + col(8 + h), very_low)
        weighted = (
            kv[:, h * dk:(h + 1) * dk].astype(jnp.float32) * jnp.exp(end_col - top)
        ).astype(jnp.bfloat16)
        own_mem[h] = dot(weighted, vv[:, h * dv:(h + 1) * dv], ((0,), (0,)))
        own_info[h:h + 1, :] = jnp.sum(weighted.astype(jnp.float32), axis=0, keepdims=True)
        own_info[heads + h:heads + h + 1, :] = jnp.broadcast_to(top, (1, dk))

    def decay(h):
        row_at = lax.broadcasted_iota(jnp.int32, (length, length), 0)
        col_at = lax.broadcasted_iota(jnp.int32, (length, length), 1)
        linked = jnp.logical_and(col(4) == row(4), row_at >= col_at)
        exponent = jnp.where(linked, col(h) - row(h) + row(8 + h), very_low)
        top = jnp.max(exponent, axis=1, keepdims=True)
        imax_scr[:, h:h + 1] = top
        prob[h] = jnp.exp(exponent - top) * factor

    def info_copy():
        return pltpu.make_async_remote_copy(
            src_ref=info_out, dst_ref=info_in, send_sem=ssend.at[heads], recv_sem=srecv.at[heads],
            device_id=up, device_id_type=MESH,
        )

    def mem_copy(h):
        return pltpu.make_async_remote_copy(
            src_ref=mem_out.at[h], dst_ref=mem_in.at[h], send_sem=ssend.at[h], recv_sem=srecv.at[h],
            device_id=up, device_id_type=MESH,
        )

    def pass_head(h):
        if h == 0:
            @pl.when(z > 0)
            def _():
                info_copy().wait_recv()

        @pl.when(z > 0)
        def _():
            mem_copy(h).wait_recv()

        @pl.when(z < Z - 1)
        def _():
            def blend(at):
                gap = jnp.where(last(4) > 0, very_low, last(at))
                shifted = info_in[heads + at:heads + at + 1, :] + gap
                top = own_info[heads + at:heads + at + 1, :]
                both = jnp.maximum(shifted, top)
                return both, jnp.exp(shifted - both), jnp.exp(top - both)

            if h == 0:
                for at in range(heads):
                    both, early, late = blend(at)
                    info_out[at:at + 1, :] = early * info_in[at:at + 1, :] + late * own_info[at:at + 1, :]
                    info_out[heads + at:heads + at + 1, :] = both
                info_copy().start()
            _, early, late = blend(h)
            mem_out[h] = (
                early[:, 0:1] * mem_in[h].astype(jnp.float32) + late[:, 0:1] * own_mem[h]
            ).astype(jnp.bfloat16)
            mem_copy(h).start()

    def start_state():
        for one in local[3:5]:
            one.wait()
        for h in range(heads):
            own_state(h)
        hand_on_first()

    def hand_on_first():
        @pl.when(z == 0)
        def _():
            mem_in[...] = jnp.zeros_like(mem_in)
            info_in[0:heads, :] = jnp.zeros((heads, dk), jnp.float32)
            info_in[heads:, :] = jnp.full((heads, dk), very_low, jnp.float32)
            for h in range(heads):
                pass_head(h)

    if not spread:
        start_state()

        @pl.when(z > 0)
        def _():
            for h in range(heads):
                pass_head(h)

        for h in range(heads):
            decay(h)
        for one in local[5:]:
            one.wait()

    def multiply(at, piece):
        part = xv[:, pl.ds(pl.multiple_of(at * rows, 128), rows)]
        acc[...] += dot(part, piece)

    if spread:
        state_steps = [pieces + heads + h for h in range(heads)]
        def places(s, low):
            q = (s + 2 * pieces) // pieces - 2
            p = (s + 2 * pieces) % pieces
            below, above = z - q, z + q
            yield below, p, jnp.logical_and(q >= low, jnp.logical_and(q < Z, below >= 0))
            yield above, p, jnp.logical_and(q >= max(low, 1), above < Z)

        def take(xx, cc, zz, p):
            @pl.when(p == pieces - 1)
            def _():
                multiply(shard(xx, cc, zz), wbuf[shard(xx, cc, zz)])

        def one_step(t, carry):
            for way, (zz, p, ok) in enumerate(places(t, 1)):
                @pl.when(ok)
                def _():
                    z_copy(way, zz, p).wait_recv()

                    @pl.when(z < Z - 1 if way == 0 else z > 0)
                    def _():
                        z_copy(way, zz, p).start()

                    x_copy(x, zz, p).start()
                    y_copy(x, zz, p, 1).start()
                    c_copy(x, c, zz, p, 0).start()

            for zz, p, ok in places(t - lag_across, 0):
                @pl.when(ok)
                def _():
                    x_copy(1 - x, zz, p).wait_recv()
                    @pl.when(jnp.logical_or(zz != z, p < pieces - early))
                    def _():
                        y_copy(1 - x, zz, p, 1).start()

                    c_copy(1 - x, c, zz, p, 0).start()

            for h in range(heads):
                @pl.when(t == pieces + h)
                def _():
                    if h == 0:
                        for one in local[3:5]:
                            one.wait()
                    own_state(h)

            @pl.when(t == pieces + heads)
            def _():
                hand_on_first()

            for h in range(heads):
                @pl.when(jnp.logical_and(t == z * 2 + state_steps[h], jnp.logical_and(z > 0, z < Z - 1)))
                def _():
                    pass_head(h)

            @pl.when(t == pieces + 1)
            def _():
                for one in local[5:]:
                    one.wait()
                acc[...] = dot(
                    xv[:, pl.ds(pl.multiple_of(shard(x, c, z) * rows, 128), rows)], wown[...]
                )

            for h in range(heads):
                @pl.when(t == 2 * pieces + h * (pieces // 2))
                def _():
                    decay(h)

            for zz, p, ok in places(t - lag_over, 1):
                @pl.when(ok)
                def _():
                    y_copy(x, zz, p, 2).wait_recv()
                    c_copy(x, c, zz, p, 2).start()
                    take(x, c, zz, p)

            for zz, p, ok in places(t - lag_over_across, 0):
                @pl.when(ok)
                def _():
                    whole = jnp.logical_and(zz == z, p >= pieces - early)

                    @pl.when(whole)
                    def _():
                        e_copy(1 - x, p).wait_recv()

                    @pl.when(jnp.logical_not(whole))
                    def _():
                        y_copy(1 - x, zz, p, 2).wait_recv()

                    c_copy(1 - x, c, zz, p, 2).start()
                    take(1 - x, c, zz, p)

            for zz, p, ok in places(t - lag_mate, 0):
                @pl.when(ok)
                def _():
                    for part in (0, 2):
                        c_copy(x, 1 - c, zz, p, part).wait_recv()
                    take(x, 1 - c, zz, p)

            for zz, p, ok in places(t - lag_mate_across, 0):
                @pl.when(ok)
                def _():
                    for part in (0, 2):
                        c_copy(1 - x, 1 - c, zz, p, part).wait_recv()
                    take(1 - x, 1 - c, zz, p)

            return carry

        lax.fori_loop(1, Z * pieces + lag_mate_across, one_step, 0)

        @pl.when(z == Z - 1)
        def _():
            for h in range(heads):
                pass_head(h)

    else:
        acc[...] = jnp.zeros_like(acc)

        def one_block(at, carry):
            multiply(at, wown[pl.ds(pl.multiple_of(at * rows, 16), rows), :])
            return carry

        lax.fori_loop(0, features // rows, one_block, 0)

    info = info_in[...]
    for h in range(heads):
        q = acc[:, h * dk:(h + 1) * dk].astype(jnp.bfloat16)
        values = vv[:, h * dv:(h + 1) * dv]
        scores = dot(q, kv[:, h * dk:(h + 1) * dk], ((1,), (1,)))
        weighted = (scores * prob[h]).astype(jnp.bfloat16)
        inner = dot(weighted, values)
        inner_den = jnp.sum(weighted.astype(jnp.float32), axis=1, keepdims=True)
        cross = dot(q, mem_in[h])
        normer = info[h:h + 1, :].astype(jnp.bfloat16).astype(jnp.float32)
        cross_den = jnp.sum(q.astype(jnp.float32) * normer, axis=1, keepdims=True)
        top = imax_scr[:, h:h + 1]
        carried = jnp.where(col(4) == 0, col(h) + info[heads + h:heads + h + 1, 0:1], very_low)
        row_max = jnp.maximum(top, carried)
        a = jnp.exp(top - row_max)
        b = jnp.exp(carried - row_max) * factor
        den = a * inner_den + b * cross_den
        inverse = 1.0 / jnp.maximum(jnp.abs(den), jnp.exp(jnp.maximum(-row_max, 0.0)))
        hidden = (a * inverse) * inner + (b * inverse) * cross
        out_ref[0, :, h * dv:(h + 1) * dv] = hidden.astype(jnp.bfloat16)

    @pl.when(z < Z - 1)
    def _():
        info_copy().wait_send()
        for h in range(heads):
            mem_copy(h).wait_send()

    if spread:
        def drain(sem, count, tall, wide):
            some = wbuf.at[0:count, 0:tall, 0:wide]
            pltpu.make_async_remote_copy(
                src_ref=some, dst_ref=some, send_sem=sem, recv_sem=sem, device_id=mate, device_id_type=MESH
            ).wait_send()

        for at in range(Z):
            @pl.when(z == at)
            def _():
                if at < Z - 1:
                    drain(zsend.at[0], at + 1, rows, A + B)
                if at > 0:
                    drain(zsend.at[1], Z - at, rows, A + B)

        drain(xsend.at[0], Z, rows, A + B)
        drain(esend.at[0], 1, early * high, A)
        drain(ysend.at[x], Z - 1, rows, A)
        drain(ysend.at[1 - x], Z * pieces - early, high, A)
        drain(csend.at[0], 2 * Z, rows, width)


def body(Z, dp, planes, normed_input, query_weight, key_vectors, value_vectors, input_gate, forget_gate, resets):
    _, length, features = normed_input.shape
    heads = input_gate.shape[1]
    width = query_weight.shape[1]
    dk = key_vectors.shape[2] // heads
    dv = value_vectors.shape[2] // heads
    spread = dp == 4 and planes == 2 and query_weight.shape[0] % 256 == 0
    if spread:
        rows = query_weight.shape[0]
        weight = query_weight
    else:
        rows = 256
        weight = lax.all_gather(query_weight, ("dp", "ctx"), axis=0, tiled=True)
    count = features // rows if spread else 1
    dma = pltpu.SemaphoreType.DMA
    hbm = pl.BlockSpec(memory_space=pltpu.HBM)
    vmem = pl.BlockSpec(memory_space=pltpu.VMEM)
    return pl.pallas_call(
        functools.partial(kernel, spread, Z, heads),
        out_shape=jax.ShapeDtypeStruct((1, length, heads * dv), jnp.bfloat16),
        in_specs=[hbm] * 7,
        out_specs=vmem,
        scratch_shapes=[
            pltpu.VMEM((2, 8, length), jnp.float32),
            pltpu.VMEM((1, length), jnp.int32),
            pltpu.VMEM((length, features), jnp.bfloat16),
            pltpu.VMEM((length, heads * dk), jnp.bfloat16),
            pltpu.VMEM((length, heads * dv), jnp.bfloat16),
            pltpu.VMEM(weight.shape, jnp.bfloat16),
            pltpu.VMEM((count, rows, width), jnp.bfloat16),
            pltpu.VMEM((length, width), jnp.float32),
            pltpu.VMEM((heads, length, length), jnp.float32),
            pltpu.VMEM((128, length), jnp.float32),
            pltpu.VMEM((length, 128), jnp.float32),
            pltpu.VMEM((length, 128), jnp.float32),
            pltpu.VMEM((heads, dk, dv), jnp.float32),
            pltpu.VMEM((2 * heads, dk), jnp.float32),
            pltpu.VMEM((heads, dk, dv), jnp.bfloat16),
            pltpu.VMEM((2 * heads, dk), jnp.float32),
            pltpu.VMEM((heads, dk, dv), jnp.bfloat16),
            pltpu.VMEM((2 * heads, dk), jnp.float32),
            dma((7,)),
            dma((2,)), dma((Z, pieces)),
            dma((1,)), dma((Z, pieces)),
            dma((1,)), dma((pieces,)),
            dma((2,)), dma((2, Z, pieces)),
            dma((1,)), dma((2, Z, pieces, 2)),
            dma((heads + 1,)), dma((heads + 1,)),
        ],
        compiler_params=pltpu.CompilerParams(
            collective_id=0, has_side_effects=True, vmem_limit_bytes=60 * 1024 * 1024
        ),
        cost_estimate=pl.CostEstimate(
            flops=2 * length * features * width, bytes_accessed=6 * 1024 * 1024, transcendentals=0
        ),
    )(normed_input, weight, key_vectors, value_vectors, input_gate, forget_gate, resets)


def solution(mesh):
    sizes = mesh.shape
    return jax.shard_map(
        functools.partial(body, sizes["ctx"], sizes["dp"], sizes["groups"]),
        mesh=mesh,
        in_specs=(
            P(("groups", "dp"), "ctx", None),
            P(("dp", "ctx"), None),
            P(("groups", "dp"), "ctx", None),
            P(("groups", "dp"), "ctx", None),
            P(("groups", "dp"), None, "ctx"),
            P(("groups", "dp"), None, "ctx"),
            P(("groups", "dp"), "ctx"),
        ),
        out_specs=P(("groups", "dp"), "ctx", None),
        check_vma=False,
    )
```

profile of v0, /device:TPU:24, one launch (start us, length us, event | category | flops | bytes accessed | tf_op | source)
XLA Modules:
  0.0 52.1 jit_solution(10519303150846542110)
XLA Ops:
  0.0 50.2 %shard_map.73 = bf16[1,256,1024]{2,1,0:T(8,128)(2,1)} custom-call(bf16[1,256,4096]{2,1,0:T(8,128)(2,1)} %x_hbm.1, bf16[256,1024]{1,0:T(8,128)(2,1)} %w_hbm.1, bf16[1,256,1024]{2,1,0:T(8,128)(2,1)} %k_hbm.1, bf16[1,256,1024]{2,1,0:T(8,128)(2,1)} %v_hbm.1, f32[1,4,256]{2,1,0:T(4,128)} %ig_hbm.1, f32[1,4,256]{2,1,0:T(4,128)} %fg_hbm.1, s32[1,256]{1,0:T(1,128)} %rs_hbm.1), custom_call_target="tpu_custom_call" | custom-call | flops 2147483648 | bytes 6291456 | tf_op jit(solution)/shard_map/pallas_call | solution.py:447
  50.2 1.9 %copy.9 = bf16[1,256,1024]{2,1,0:T(8,128)(2,1)} copy(bf16[1,256,1024]{2,1,0:T(8,128)(2,1)} %shard_map.73) | data formatting | bytes 1048576
where the time goes:
time: 52.2 us; the launch traced here: 52.1 us
  Pallas kernels  50.2 us (96%)
  local copies, waits for them, and re-layouts  1.87 us (4%)
    pallas_call x1, Pallas kernels, body(): pl.pallas_call(functools.partial(kernel, spread, Z, heads), out_shape=jax...  50.2 us
    unnamed x1, local copies, waits for them, and re-layouts  1.87 us

commit v1 on v0

--- a/solution.py
+++ b/solution.py
@@ -227,9 +227,7 @@
             one.wait()
         for h in range(heads):
             own_state(h)
-        hand_on_first()
-
-    def hand_on_first():
+
         @pl.when(z == 0)
         def _():
             mem_in[...] = jnp.zeros_like(mem_in)
@@ -256,7 +254,7 @@
         acc[...] += dot(part, piece)
 
     if spread:
-        state_steps = [pieces + heads + h for h in range(heads)]
+        state_steps = [-(-2 * pieces * (h + 1) // 5) for h in range(heads)]
         def places(s, low):
             q = (s + 2 * pieces) // pieces - 2
             p = (s + 2 * pieces) % pieces
@@ -294,24 +292,13 @@
                     c_copy(1 - x, c, zz, p, 0).start()
 
             for h in range(heads):
-                @pl.when(t == pieces + h)
-                def _():
-                    if h == 0:
-                        for one in local[3:5]:
-                            one.wait()
-                    own_state(h)
-
-            @pl.when(t == pieces + heads)
-            def _():
-                hand_on_first()
-
-            for h in range(heads):
-                @pl.when(jnp.logical_and(t == z * 2 + state_steps[h], jnp.logical_and(z > 0, z < Z - 1)))
+                @pl.when(jnp.logical_and(t == z * pieces + state_steps[h], jnp.logical_and(z > 0, z < Z - 1)))
                 def _():
                     pass_head(h)
 
-            @pl.when(t == pieces + 1)
-            def _():
+            @pl.when(t == lag_across + 1)
+            def _():
+                start_state()
                 for one in local[5:]:
                     one.wait()
                 acc[...] = dot(
@@ -319,7 +306,7 @@
                 )
 
             for h in range(heads):
-                @pl.when(t == 2 * pieces + h * (pieces // 2))
+                @pl.when(t == pieces + 1 + h * (pieces // 2))
                 def _():
                     decay(h)
 

time: 52.2 us -> 51.8 us (level)
  Pallas kernels: 50.2 us -> 49.6 us
    pallas_call x1, Pallas kernels: 50.2 us -> 49.6 us  [body(): pl.pallas_call(functools.partial(kernel, spread, Z, heads), out_shape=jax...]
where the time goes in v1:
time: 51.8 us; the launch traced here: 51.4 us
  Pallas kernels  49.6 us (96%)
  local copies, waits for them, and re-layouts  1.87 us (4%)
    pallas_call x1, Pallas kernels, body(): pl.pallas_call(functools.partial(kernel, spread, Z, heads), out_shape=jax...  49.6 us
    unnamed x1, local copies, waits for them, and re-layouts  1.87 us

profile of v1, /device:TPU:24, one launch (start us, length us, event | category | flops | bytes accessed | tf_op | source)
XLA Modules:
  0.0 51.4 jit_solution(8319731356966535145)
XLA Ops:
  0.0 49.6 %shard_map.73 = bf16[1,256,1024]{2,1,0:T(8,128)(2,1)} custom-call(bf16[1,256,4096]{2,1,0:T(8,128)(2,1)} %x_hbm.1, bf16[256,1024]{1,0:T(8,128)(2,1)} %w_hbm.1, bf16[1,256,1024]{2,1,0:T(8,128)(2,1)} %k_hbm.1, bf16[1,256,1024]{2,1,0:T(8,128)(2,1)} %v_hbm.1, f32[1,4,256]{2,1,0:T(4,128)} %ig_hbm.1, f32[1,4,256]{2,1,0:T(4,128)} %fg_hbm.1, s32[1,256]{1,0:T(1,128)} %rs_hbm.1), custom_call_target="tpu_custom_call" | custom-call | flops 2147483648 | bytes 6291456 | tf_op jit(solution)/shard_map/pallas_call | solution.py:434
  49.6 1.9 %copy.9 = bf16[1,256,1024]{2,1,0:T(8,128)(2,1)} copy(bf16[1,256,1024]{2,1,0:T(8,128)(2,1)} %shard_map.73) | data formatting | bytes 1048576
